TPU v7x, 128 devices: a whole 4x4x4 slice. The times are simulated.
128 devices in a mesh: depth: 2 (over core), rows: 2 (over x_hi), shots: 32 (over z, y, x_lo).
Axes of the slice: x: 4 (x_hi: 2, x_lo: 2; x = x_hi * 2 + x_lo), y: 4, z: 4, core: 2. Of those that a mesh axis runs over, the one named last changes fastest.
Arguments:
- sources: float32 [2, 2, 1024, 4096], P('depth', None, 'rows', 'shots'), may hold values from -6 to 6
- factor: float32 [2, 2, 1024, 1024], P('depth', None, ('rows', 'shots')), may hold values from -0.09375 to 0.09375
- block_mask: int32 [2, 2, 8, 8], P('depth'), may hold values 0 or 1
- inverse_diagonal: float32 [2, 2, 1024, 1024], P('depth', None, None, 'rows'), may hold values from -1.2 to 1.2, as said below
Outputs:
- solution: float32 [2, 2, 1024, 4096], P('depth', None, 'rows', 'shots')
Inputs may be any that keep to these rules, and one draw needn't show every extreme that they name: Each block inverse_diagonal[d, m] is lower triangular with diagonal entries between 0.8 and 1.2.
All inputs are finite; a program needn't handle non-finite values. No bound on the sum of `block_mask` on one device may be relied on, other than what follows from the above.
Results may differ from a plain program's by a relative error of at most 0.0001.
Values sent between devices are 32-bit elements; how exact they have to be, the bound alone decides.
A program may use at most 64 MiB of HBM per device.

v0:
```python
import jax
import jax.numpy as jnp
from jax import lax
from jax.sharding import PartitionSpec as P


def mask_rows(factor_rows, block_mask, row_start, block_size):
    row_total = factor_rows.shape[1]
    block_count = block_mask.shape[3]
    row_blocks = (row_start + jnp.arange(row_total, dtype=jnp.int32)) // block_size
    row_select = (row_blocks[:, None] == jnp.arange(block_count, dtype=jnp.int32)[None, :]).astype(
        jnp.float32
    )
    row_masks = jnp.einsum("rk,pkc->prc", row_select, block_mask[0].astype(jnp.float32))
    return factor_rows * jnp.repeat(row_masks, block_size, axis=2)


def product(spec, left, right):
    return jnp.einsum(
        spec, left, right, precision=lax.Precision.HIGH, preferred_element_type=jnp.float32
    )


def per_device(sources, factor, block_mask, inverse_diagonal):
    shot_index = lax.axis_index("shots")
    rows_index = lax.axis_index("rows")
    thin_rows = factor.shape[2]
    full_width = factor.shape[3]
    block_size = full_width // block_mask.shape[3]
    row_start = (rows_index * lax.axis_size("shots") + shot_index) * thin_rows
    masked = mask_rows(factor[0], block_mask, row_start, block_size)
    tiles = lax.all_gather(masked, "shots", axis=1, tiled=True)
    low = lax.psum(product("rs,sn->rn", inverse_diagonal[0, 0], sources[0, 0]), "rows")
    update = product("trs,sn->trn", tiles, low)
    own = sources[0, 1] - lax.psum_scatter(update, "depth", scatter_dimension=0, tiled=True)[0]
    high = lax.psum(product("rs,sn->rn", inverse_diagonal[0, 1], own), "rows")
    top = product("sr,sn->rn", inverse_diagonal[0, 1], high)
    tops = lax.all_gather(top[None], "depth", axis=0, tiled=True)
    target = low - lax.psum(product("trs,trn->sn", tiles, tops), "rows")
    bottom = product("sr,sn->rn", inverse_diagonal[0, 0], target)
    return jnp.stack([bottom, top])[None]


def solution(mesh):
    placed = (
        P("depth", None, "rows", "shots"),
        P("depth", None, ("rows", "shots"), None),
        P("depth", None, None, None),
        P("depth", None, None, "rows"),
    )
    return jax.shard_map(
        per_device,
        mesh=mesh,
        in_specs=placed,
        out_specs=P("depth", None, "rows", "shots"),
        check_vma=False,
    )
```

profile of v0, /device:TPU:1, one launch (start us, length us, event | category | flops | bytes accessed | tf_op | source)
XLA Modules:
  0.0 303.1 jit_solution(8039582276913375339)
XLA Ops:
  7.4 0.0 all-reduce.4.cloned.1.call-start
  7.4 3.4 %fusion.6 = f32[1024,128]{1,0:T(8,128)} fusion(f32[1,2,1024,512]{3,2,1,0:T(8,128)} %param.7, f32[1,2,512,128]{3,2,1,0:T(8,128)} %param.4), kind=kOutput, calls=%fused_computation.6 | convolution fusion | flops 402653184 | bytes 2883584 | tf_op jit(solution)/shard_map/rs,sn->rn/dot_general | solution.py:19
  10.8 0.0 all-reduce.4.cloned.1.call-update
  10.8 0.0 all-gather.3.cloned.1.call-start
  10.8 0.7 convert_bitcast_fusion
  11.6 0.1 copy.5
  11.7 0.1 convolution_bitcast_fusion.1
  11.8 0.1 copy.6
  11.9 0.1 broadcast_in_dim.11
  12.0 1.6 bitcast_multiply_fusion
  13.6 0.0 all-gather.3.cloned.1.call-update
  13.6 0.0 reduce-scatter.2.cloned.1.call-start
  13.7 38.2 %all-reduce.4.cloned.1.call-done = f32[1024,128]{1,0:T(8,128)} async-done(((f32[1024,128]{1,0:T(8,128)}), f32[1024,128]{1,0:T(8,128)}) %all-reduce.4.cloned.1.call-update) | async-done | bytes 524304 | tf_op jit(solution)/shard_map/psum | solution.py:33
  51.8 116.8 %all-gather.3.cloned.1.call-done = f32[2,512,1024]{2,1,0:T(8,128)} async-done(((f32[2,16,1024]{2,1,0:T(8,128)}), f32[2,512,1024]{2,1,0:T(8,128)}) %all-gather.3.cloned.1.call-update) | async-done | bytes 4194320 | tf_op jit(solution)/shard_map/all_gather | solution.py:32
  168.6 4.9 %fusion.18 = f32[2,512,128]{2,1,0:T(8,128)} fusion(f32[2,512,1024]{2,1,0:T(8,128)} %all-gather.3.cloned.1.call-done, f32[1024,128]{1,0:T(8,128)} %all-reduce.4.cloned.1.call-done), kind=kOutput, calls=%fused_computation.17 | convolution fusion | flops 805306368 | bytes 5242880 | tf_op jit(solution)/shard_map/trs,sn->trn/dot_general | solution.py:19
  173.5 0.0 reduce-scatter.2.cloned.1.call-update
  173.5 0.0 all-reduce.6.cloned.1.call-start
  173.6 29.7 %reduce-scatter.2.cloned.1.call-done = f32[1,512,128]{2,1,0:T(8,128)} async-done(((f32[2,512,128]{2,1,0:T(8,128)}), f32[1,512,128]{2,1,0:T(8,128)}) %reduce-scatter.2.cloned.1.call-update) | async-done | bytes 262160 | tf_op jit(solution)/shard_map/reduce_scatter | solution.py:35
  203.3 0.0 copy-done.1
  203.3 3.7 %fusion.12 = f32[1024,128]{0,1:T(8,128)} fusion(f32[1,2,1024,512]{3,2,1,0:T(8,128)} %param.7, f32[1,512,128]{2,1,0:T(8,128)} %reduce-scatter.2.cloned.1.call-done, f32[1,2,512,128]{3,2,1,0:T(8,128)S(1)} %copy-done.1), kind=kOutput, calls=%fused_computation.12 | convolution fusion | flops 402718720 | bytes 3145728 | tf_op jit(solution)/shard_map/rs,sn->rn/dot_general | solution.py:19
  207.0 0.0 all-reduce.6.cloned.1.call-update
  207.0 0.0 all-reduce.8.cloned.1.call-start
  207.0 37.6 %all-reduce.6.cloned.1.call-done = f32[1024,128]{0,1:T(8,128)} async-done(((f32[1024,128]{0,1:T(8,128)}), f32[1024,128]{0,1:T(8,128)}) %all-reduce.6.cloned.1.call-update) | async-done | bytes 524304 | tf_op jit(solution)/shard_map/psum | solution.py:36
  244.7 2.5 fusion
  247.2 0.0 copy-start
  247.2 2.6 all-gather
  249.8 0.2 copy.9
  250.0 6.4 %convolution_bitcast_fusion = f32[1024,128]{1,0:T(8,128)} fusion(f32[2,512,1024]{2,1,0:T(8,128)} %all-gather.3.cloned.1.call-done, f32[2,512,128]{2,1,0:T(8,128)S(1)} %bitcast.63), kind=kOutput, calls=%fused_computation.13 | convolution fusion | flops 805306368 | bytes 5242880 | tf_op jit(solution)/shard_map/trs,trn->sn/dot_general | solution.py:19
  256.4 0.0 all-reduce.8.cloned.1.call-update
  256.4 36.0 %all-reduce.8.cloned.1.call-done = f32[1024,128]{1,0:T(8,128)} async-done(((f32[1024,128]{1,0:T(8,128)}), f32[1024,128]{1,0:T(8,128)}) %all-reduce.8.cloned.1.call-update) | async-done | bytes 524304 | tf_op jit(solution)/shard_map/psum | solution.py:39
  292.4 2.5 fusion.15
  295.0 1.0 copy.7
  (5 shorter events, 0.1 us)
Async XLA Ops:
  7.4 44.5 %all-reduce.4.cloned.1.call-start = ((), (), s32[]{:S(2)}) async-start(), calls=%async_computation.1 | async-start | bytes 1048576 | tf_op jit(solution)/shard_map/psum | solution.py:33
  10.8 192.5 %copy-start.1 = (f32[1,2,512,128]{3,2,1,0:T(8,128)S(1)}, f32[1,2,512,128]{3,2,1,0:T(8,128)}, u32[]{:S(2)}) copy-start(f32[1,2,512,128]{3,2,1,0:T(8,128)} %param.4) | copy-start | bytes 1572868
  10.8 157.8 %all-gather.3.cloned.1.call-start = ((), (), s32[]{:S(2)}) async-start(), calls=%async_computation.2 | async-start | bytes 4325376 | tf_op jit(solution)/shard_map/all_gather | solution.py:32
  13.6 189.7 %reduce-scatter.2.cloned.1.call-start = ((), (), s32[]{:S(2)}) async-start(), calls=%async_computation.3 | async-start | bytes 786432 | tf_op jit(solution)/shard_map/reduce_scatter | solution.py:35
  173.5 71.2 %all-reduce.6.cloned.1.call-start = ((), (), s32[]{:S(2)}) async-start(), calls=%async_computation.4 | async-start | bytes 1048576 | tf_op jit(solution)/shard_map/psum | solution.py:36
  207.0 85.4 %all-reduce.8.cloned.1.call-start = ((), (), s32[]{:S(2)}) async-start(), calls=%async_computation.5 | async-start | bytes 1048576 | tf_op jit(solution)/shard_map/psum | solution.py:39
  247.2 45.2 %copy-start = (f32[1024,128]{1,0:T(8,128)S(1)}, f32[1024,128]{1,0:T(8,128)}, u32[]{:S(2)}) copy-start(f32[1024,128]{1,0:T(8,128)} %all-reduce.4.cloned.1.call-done) | copy-start | bytes 1572868
Sparse Core Ops, SparseCore 0:
  10.9 40.8 all-reduce.3
  173.6 29.5 reduce-scatter.1
  207.1 37.5 all-reduce.5
  256.5 35.7 all-reduce.7
Sparse Core Ops, SparseCore 1:
  13.7 154.9 all-gather.2
where the time goes:
time: 303 us
  waiting for transfers between devices  258 us (85%)
  matrix products  23.5 us (8%)
  between operations  14.6 us (5%)
    all_gather x1, waiting for transfers between devices, per_device(): tiles = lax.all_gather(masked, 'shots', axis=1, tiled=True)  117 us
    psum x1, waiting for transfers between devices, per_device(): lax.psum(product('rs,sn->rn', inverse_diagonal[0, 0], sources[0, 0]), 'ro...  38.2 us
    psum x1, waiting for transfers between devices, per_device(): high = lax.psum(product('rs,sn->rn', inverse_diagonal[0, 1], own), 'rows')  37.6 us
    psum x1, waiting for transfers between devices, per_device(): target = low - lax.psum(product('trs,trn->sn', tiles, tops), 'rows')  36 us
    reduce_scatter x1, waiting for transfers between devices, per_device(): lax.psum_scatter(update, 'depth', scatter_dimension=0, tiled=True)[0]  29.7 us
    dot_general x6, matrix products, product(): jnp.einsum(spec, left, right, precision=lax.Precision.HIGH, preferred_ele...  23.4 us
  transfers between devices with their start and end apart: 5, of which 5 were waited for; matrix products, arithmetic and copies ran while one was open for 1% of the time, Pallas kernels for 0%

commit v1 on v0

--- a/solution.py
+++ b/solution.py
@@ -29,7 +29,9 @@
     block_size = full_width // block_mask.shape[3]
     row_start = (rows_index * lax.axis_size("shots") + shot_index) * thin_rows
     masked = mask_rows(factor[0], block_mask, row_start, block_size)
-    tiles = lax.all_gather(masked, "shots", axis=1, tiled=True)
+    tiles = jnp.concatenate(
+        lax.all_to_all(jnp.stack([masked] * lax.axis_size("shots")), "shots", 0, 0), axis=1
+    )
     low = lax.psum(product("rs,sn->rn", inverse_diagonal[0, 0], sources[0, 0]), "rows")
     update = product("trs,sn->trn", tiles, low)
     own = sources[0, 1] - lax.psum_scatter(update, "depth", scatter_dimension=0, tiled=True)[0]

time: 303 us -> 206 us (0.68)
  waiting for transfers between devices: 258 us -> 145 us
  starting transfers between devices: 0.17 us -> 10.2 us
  local copies, waits for them, and re-layouts: 1.48 us -> 8.65 us
    all_gather x1 -> x0, waiting for transfers between devices: 117 us -> none  [per_device(): tiles = lax.all_gather(masked, 'shots', axis=1, tiled=True)]
    all_to_all x0 -> x1, waiting for transfers between devices: none -> 59 us  [per_device(): lax.all_to_all(jnp.stack([masked] * lax.axis_size('shots')), 'shots', 0, 0)]
    psum x1, waiting for transfers between devices: 38.2 us -> 0.01 us  [per_device(): lax.psum(product('rs,sn->rn', inverse_diagonal[0, 0], sources[0, 0]), 'ro...]
    reduce_scatter x1, waiting for transfers between devices: 29.7 us -> 12.6 us  [per_device(): lax.psum_scatter(update, 'depth', scatter_dimension=0, tiled=True)[0]]
    all_to_all x0 -> x1, starting transfers between devices: none -> 10.1 us  [per_device(): lax.all_to_all(jnp.stack([masked] * lax.axis_size('shots')), 'shots', 0, 0)]
    reshape x0 -> x1, local copies, waits for them, and re-layouts: none -> 4.71 us  [per_device(): jnp.concatenate(lax.all_to_all(jnp.stack([masked] * lax.axis_size('shots'...]
  transfers between devices with their start and end apart: 5 -> 5, of which waited for: 5 -> 4; matrix products, arithmetic and copies ran while one was open for 1% -> 4% of each run, Pallas kernels for 0% -> 0%
where the time goes in v1:
time: 206 us; the launch traced here: 205 us
  waiting for transfers between devices  145 us (70%)
  matrix products  23.5 us (11%)
  between operations  13.2 us (6%)
  starting transfers between devices  10.2 us (5%)
  local copies, waits for them, and re-layouts  8.65 us (4%)
  blocking collectives  2.61 us (1%)
    all_to_all x1, waiting for transfers between devices, per_device(): lax.all_to_all(jnp.stack([masked] * lax.axis_size('shots')), 'shots', 0, 0)  59 us
    psum x1, waiting for transfers between devices, per_device(): high = lax.psum(product('rs,sn->rn', inverse_diagonal[0, 1], own), 'rows')  37.6 us
    psum x1, waiting for transfers between devices, per_device(): target = low - lax.psum(product('trs,trn->sn', tiles, tops), 'rows')  36 us
    dot_general x6, matrix products, product(): jnp.einsum(spec, left, right, precision=lax.Precision.HIGH, preferred_ele...  23.4 us
    reduce_scatter x1, waiting for transfers between devices, per_device(): lax.psum_scatter(update, 'depth', scatter_dimension=0, tiled=True)[0]  12.6 us
    all_to_all x1, starting transfers between devices, per_device(): lax.all_to_all(jnp.stack([masked] * lax.axis_size('shots')), 'shots', 0, 0)  10.1 us
    reshape x1, local copies, waits for them, and re-layouts, per_device(): jnp.concatenate(lax.all_to_all(jnp.stack([masked] * lax.axis_size('shots'...  4.71 us
  transfers between devices with their start and end apart: 5, of which 4 were waited for; matrix products, arithmetic and copies ran while one was open for 4% of the time, Pallas kernels for 0%

profile of v1, /device:TPU:1, one launch (start us, length us, event | category | flops | bytes accessed | tf_op | source)
XLA Modules:
  0.0 205.1 jit_solution(12994076606216050788)
XLA Ops:
  6.5 0.7 convert_bitcast_fusion
  7.2 0.1 copy.8
  7.3 0.1 convolution_bitcast_fusion.1
  7.5 0.1 copy.9
  7.5 0.1 broadcast_in_dim.11
  7.7 0.9 multiply_bitcast_fusion
  8.6 2.5 %stack.9 = f32[32,2,16,1024]{3,2,1,0:T(8,128)} broadcast(f32[2,16,1024]{2,1,0:T(8,128)S(1)} %multiply_bitcast_fusion), dimensions={1,2,3} | broadcast | bytes 4325376 | tf_op jit(solution)/shard_map/stack | solution.py:33
  11.1 10.1 %all-to-all-start = ((f32[32,2,16,1024]{3,2,1,0:T(8,128)}), f32[32,2,16,1024]{3,2,1,0:T(8,128)}, u32[]{:S(2)}, u32[]{:S(2)}) async-start(f32[32,2,16,1024]{3,2,1,0:T(8,128)} %stack.9), calls=%async_computation | async-start | bytes 8388608 | tf_op jit(solution)/shard_map/all_to_all | solution.py:33
  21.1 0.0 all-reduce.4.cloned.1.call-start
  21.2 0.0 copy-done.1
  21.2 3.4 %fusion.6 = f32[1024,128]{1,0:T(8,128)} fusion(f32[1,2,1024,512]{3,2,1,0:T(8,128)} %param.7, f32[1,2,512,128]{3,2,1,0:T(8,128)S(1)} %copy-done.1), kind=kOutput, calls=%fused_computation.6 | convolution fusion | flops 402653184 | bytes 2883584 | tf_op jit(solution)/shard_map/rs,sn->rn/dot_general | solution.py:19
  24.6 0.0 all-reduce.4.cloned.1.call-update
  24.6 0.0 reduce-scatter.2.cloned.1.call-start
  24.6 59.0 %all-to-all-done = f32[32,2,16,1024]{3,2,1,0:T(8,128)} async-done(((f32[32,2,16,1024]{3,2,1,0:T(8,128)}), f32[32,2,16,1024]{3,2,1,0:T(8,128)}, u32[]{:S(2)}, u32[]{:S(2)}) %all-to-all-start) | async-done | bytes 4194336 | tf_op jit(solution)/shard_map/all_to_all | solution.py:33
  83.7 4.7 %copy.10 = f32[2,32,16,1024]{3,2,1,0:T(8,128)} copy(f32[2,32,16,1024]{3,2,0,1:T(8,128)} %bitcast.8) | data formatting | bytes 8388608 | tf_op jit(solution)/shard_map/reshape | solution.py:32
  88.4 4.9 %fusion.18 = f32[2,512,128]{2,1,0:T(8,128)} fusion(f32[2,512,1024]{2,1,0:T(8,128)} %bitcast.63, f32[1024,128]{1,0:T(8,128)} %all-reduce.4.cloned.1.call-done), kind=kOutput, calls=%fused_computation.17 | convolution fusion | flops 805306368 | bytes 5242880 | tf_op jit(solution)/shard_map/trs,sn->trn/dot_general | solution.py:19
  93.3 0.0 reduce-scatter.2.cloned.1.call-update
  93.3 0.0 all-reduce.6.cloned.1.call-start
  93.4 12.6 %reduce-scatter.2.cloned.1.call-done = f32[1,512,128]{2,1,0:T(8,128)} async-done(((f32[2,512,128]{2,1,0:T(8,128)}), f32[1,512,128]{2,1,0:T(8,128)}) %reduce-scatter.2.cloned.1.call-update) | async-done | bytes 262160 | tf_op jit(solution)/shard_map/reduce_scatter | solution.py:37
  105.9 3.7 %fusion.12 = f32[1024,128]{0,1:T(8,128)} fusion(f32[1,2,1024,512]{3,2,1,0:T(8,128)} %param.7, f32[1,512,128]{2,1,0:T(8,128)} %reduce-scatter.2.cloned.1.call-done, f32[1,2,512,128]{3,2,1,0:T(8,128)S(1)} %copy-done.1), kind=kOutput, calls=%fused_computation.12 | convolution fusion | flops 402718720 | bytes 3145728 | tf_op jit(solution)/shard_map/rs,sn->rn/dot_general | solution.py:19
  109.6 0.0 all-reduce.6.cloned.1.call-update
  109.6 0.0 all-reduce.8.cloned.1.call-start
  109.7 37.6 %all-reduce.6.cloned.1.call-done = f32[1024,128]{0,1:T(8,128)} async-done(((f32[1024,128]{0,1:T(8,128)}), f32[1024,128]{0,1:T(8,128)}) %all-reduce.6.cloned.1.call-update) | async-done | bytes 524304 | tf_op jit(solution)/shard_map/psum | solution.py:38
  147.3 2.5 %fusion = f32[128,512]{1,0:T(8,128)S(1)} fusion(f32[1024,128]{0,1:T(8,128)} %all-reduce.6.cloned.1.call-done, f32[1,2,1024,512]{3,2,1,0:T(8,128)} %param.7), kind=kOutput, calls=%fused_computation | convolution fusion | flops 402653184 | bytes 2883584 | tf_op jit(solution)/shard_map/sr,sn->rn/dot_general | solution.py:19
  149.8 0.0 copy-start
  149.8 2.6 %all-gather = f32[1024,128]{0,1:T(8,128)S(1)} all-gather(f32[512,128]{0,1:T(8,128)S(1)} %bitcast.65), channel_id=2, replica_groups=mesh['depth'=2,'rows'=2,'shots'=32] {'depth'}, dimensions={0}, use_global_device_ids=true | all-gather | bytes 786432 | tf_op jit(solution)/shard_map/all_gather | solution.py:40
  152.4 0.2 copy.13
  152.6 6.4 %convolution_bitcast_fusion = f32[1024,128]{1,0:T(8,128)} fusion(f32[2,512,1024]{2,1,0:T(8,128)} %bitcast.64, f32[2,512,128]{2,1,0:T(8,128)S(1)} %bitcast.67), kind=kOutput, calls=%fused_computation.13 | convolution fusion | flops 805306368 | bytes 5242880 | tf_op jit(solution)/shard_map/trs,trn->sn/dot_general | solution.py:19
  159.1 0.0 all-reduce.8.cloned.1.call-update
  159.1 36.0 %all-reduce.8.cloned.1.call-done = f32[1024,128]{1,0:T(8,128)} async-done(((f32[1024,128]{1,0:T(8,128)}), f32[1024,128]{1,0:T(8,128)}) %all-reduce.8.cloned.1.call-update) | async-done | bytes 524304 | tf_op jit(solution)/shard_map/psum | solution.py:41
  195.0 2.5 %fusion.15 = f32[1,512,128]{1,2,0:T(8,128)S(1)} fusion(f32[1,2,1024,512]{3,2,1,0:T(8,128)} %param.7, f32[1024,128]{1,0:T(8,128)S(1)} %copy-done, f32[1024,128]{1,0:T(8,128)} %all-reduce.8.cloned.1.call-done), kind=kOutput, calls=%fused_computation.14 | convolution fusion | flops 402784256 | bytes 3407872 | tf_op jit(solution)/shard_map/sr,sn->rn/dot_general | solution.py:19
  197.6 1.0 copy.11
  (6 shorter events, 0.1 us)
Async XLA Ops:
  11.1 10.1 %copy-start.1 = (f32[1,2,512,128]{3,2,1,0:T(8,128)S(1)}, f32[1,2,512,128]{3,2,1,0:T(8,128)}, u32[]{:S(2)}) copy-start(f32[1,2,512,128]{3,2,1,0:T(8,128)} %param.4) | copy-start | bytes 1572868
  11.1 72.6 %all-to-all-start = ((f32[32,2,16,1024]{3,2,1,0:T(8,128)}), f32[32,2,16,1024]{3,2,1,0:T(8,128)}, u32[]{:S(2)}, u32[]{:S(2)}) async-start(f32[32,2,16,1024]{3,2,1,0:T(8,128)} %stack.9), calls=%async_computation | async-start | bytes 8388608 | tf_op jit(solution)/shard_map/all_to_all | solution.py:33
  21.1 67.3 %all-reduce.4.cloned.1.call-start = ((), (), s32[]{:S(2)}) async-start(), calls=%async_computation.2 | async-start | bytes 1048576 | tf_op jit(solution)/shard_map/psum | solution.py:35
  24.6 81.3 %reduce-scatter.2.cloned.1.call-start = ((), (), s32[]{:S(2)}) async-start(), calls=%async_computation.3 | async-start | bytes 786432 | tf_op jit(solution)/shard_map/reduce_scatter | solution.py:37
  93.3 54.0 %all-reduce.6.cloned.1.call-start = ((), (), s32[]{:S(2)}) async-start(), calls=%async_computation.4 | async-start | bytes 1048576 | tf_op jit(solution)/shard_map/psum | solution.py:38
  109.6 85.4 %all-reduce.8.cloned.1.call-start = ((), (), s32[]{:S(2)}) async-start(), calls=%async_computation.5 | async-start | bytes 1048576 | tf_op jit(solution)/shard_map/psum | solution.py:41
  149.8 45.2 %copy-start = (f32[1024,128]{1,0:T(8,128)S(1)}, f32[1024,128]{1,0:T(8,128)}, u32[]{:S(2)}) copy-start(f32[1024,128]{1,0:T(8,128)} %all-reduce.4.cloned.1.call-done) | copy-start | bytes 1572868
Sparse Core Ops, SparseCore 0:
  24.7 50.2 all-reduce.3
  93.4 12.4 reduce-scatter.1
  109.8 37.5 all-reduce.5
  159.2 35.7 all-reduce.7
